TPU v7x, 32 devices: a whole 2x2x4 slice. The times are simulated.
32 devices in a mesh: tile: 8 (over y, x, core), head: 4 (over z).
Axes of the slice: x: 2, y: 2, z: 4, core: 2. Of those that a mesh axis runs over, the one named last changes fastest.
Arguments:
- bott: bfloat16 [16, 128, 1024], P('tile', 'head'), may hold values from -10 to 10
- norm_gain: float32 [1024], replicated, may hold values from 0.1 to 1.9
- w_qkv: bfloat16 [3, 1024, 1024], P(None, None, 'head'), may hold values from -1 to 1
- w_out: bfloat16 [1024, 1024], P('head'), may hold values from -3 to 3
- dw_weight: float32 [3, 3, 1024], replicated, may hold values from -2 to 2
- join_bias: float32 [1024], replicated, may hold values from -3 to 3
- w_join: bfloat16 [1024, 1024], replicated, may hold values from -0.1875 to 0.1875
Outputs:
- joined: bfloat16 [16, 128, 1024], P('tile', 'head')
All inputs are finite; a program needn't handle non-finite values.
Results may differ from a plain program's by a relative error of at most 0.02.
Values may be sent and summed in bfloat16 or wider, within the bound.
A program may use at most 128 MiB of HBM per device.

v0:
```python
import math
import jax
import jax.numpy as jnp
from jax import lax
from jax.sharding import PartitionSpec as P

HEADS = 16


def with_halo(x, sides, width):
    for axis, dim in sides:
        size, length = (lax.axis_size(axis), x.shape[dim])
        up = [(i, (i + 1) % size) for i in range(size - 1)]
        down = [(j, i) for i, j in up]
        last = lax.slice_in_dim(x, length - width, length, axis=dim)
        leading = lax.slice_in_dim(x, 0, width, axis=dim)
        before = lax.ppermute(last, axis, up)
        after = lax.ppermute(leading, axis, down)
        x = jnp.concatenate([before, x, after], axis=dim)
    return x


def fold_blocks(state, queries, key_piece, value_piece, scale):
    count, heads_here, head_dim = key_piece.shape
    block = math.gcd(count, 2048)
    key_blocks = key_piece.reshape(count // block, block, heads_here, head_dim)
    value_blocks = value_piece.reshape(count // block, block, heads_here, head_dim)

    def one_block(inner, pair):
        maxes, totals, summed = inner
        key_block, value_block = pair
        scores = (
            jnp.einsum("qhe,khe->hqk", queries, key_block, preferred_element_type=jnp.float32)
            * scale
        )
        new_max = jnp.maximum(maxes, jnp.max(scores, axis=-1))
        weights = jnp.exp(scores - new_max[..., None])
        decay = jnp.exp(maxes - new_max)
        totals = totals * decay + jnp.sum(weights, axis=-1)
        summed = summed * decay[..., None] + jnp.einsum(
            "hqk,khe->hqe",
            weights.astype(jnp.bfloat16),
            value_block,
            preferred_element_type=jnp.float32,
        )
        return ((new_max, totals, summed), None)

    return lax.scan(one_block, state, (key_blocks, value_blocks))[0]


def empty_state(heads_here, query_count, head_dim):
    return (
        jnp.full((heads_here, query_count), -1e30, jnp.float32),
        jnp.zeros((heads_here, query_count), jnp.float32),
        jnp.zeros((heads_here, query_count, head_dim), jnp.float32),
    )


def per_device(bott, norm_gain, w_qkv, w_out, dw_weight, join_bias, w_join):
    rows, cols_dev, width = bott.shape
    values = bott.astype(jnp.float32)
    normed = (
        values * lax.rsqrt(jnp.mean(values * values, axis=-1, keepdims=True) + 1e-06) * norm_gain
    ).astype(jnp.bfloat16)
    all_heads = jnp.einsum(
        "rcd,jde->jcre",
        normed,
        lax.all_gather(w_qkv, "head", axis=2, tiled=True),
        preferred_element_type=jnp.float32,
    ).astype(jnp.bfloat16)
    projected = lax.all_to_all(all_heads, "head", split_axis=3, concat_axis=1, tiled=True)
    columns = projected.shape[1]
    local_width = projected.shape[3]
    head_dim = width // HEADS
    local_heads = local_width // head_dim
    seq_local = columns * rows
    scale = 1.0 / head_dim**0.5
    queries = projected[0].reshape(seq_local, local_heads, head_dim)
    keys = projected[1].reshape(seq_local, local_width)
    vals = projected[2].reshape(seq_local, local_width)
    start_state = empty_state(local_heads, seq_local, head_dim)
    key_piece = lax.all_gather(keys, "tile", axis=0, tiled=True)
    value_piece = lax.all_gather(vals, "tile", axis=0, tiled=True)
    count = key_piece.shape[0]
    maxes, totals, summed = fold_blocks(
        start_state,
        queries,
        key_piece.reshape(count, local_heads, head_dim),
        value_piece.reshape(count, local_heads, head_dim),
        scale,
    )
    attended = (summed / totals[..., None]).astype(jnp.bfloat16)
    attended = jnp.transpose(attended, (1, 0, 2)).reshape(columns, rows, local_width)
    mixed = lax.psum_scatter(
        jnp.einsum("crh,hd->crd", attended, w_out, preferred_element_type=jnp.float32).astype(
            jnp.bfloat16
        ),
        "head",
        scatter_dimension=0,
        tiled=True,
    ).astype(jnp.float32)
    context = (values + jnp.transpose(mixed, (1, 0, 2))).astype(jnp.bfloat16)
    padded = with_halo(context, (("tile", 0), ("head", 1)), 1).astype(jnp.float32)
    conv = jnp.zeros((rows, cols_dev, width), jnp.float32)
    for i in range(3):
        for j in range(3):
            conv = conv + padded[i : i + rows, j : j + cols_dev] * dw_weight[i, j]
    hidden = jax.nn.gelu(conv + join_bias).astype(jnp.bfloat16)
    projected_out = jnp.einsum("rcd,de->rce", hidden, w_join, preferred_element_type=jnp.float32)
    return (context.astype(jnp.float32) + projected_out).astype(jnp.bfloat16)


def solution(mesh):
    placed = (P("tile", "head", None), P(), P(None, None, "head"), P("head", None), P(), P(), P())
    return jax.shard_map(
        per_device, mesh=mesh, in_specs=placed, out_specs=P("tile", "head", None), check_vma=False
    )
```

profile of v0, /device:TPU:11, one launch (start us, length us, event | category | flops | bytes accessed | tf_op | source)
XLA Modules:
  0.0 259.9 jit_solution(10153033517805802378)
XLA Ops:
  6.5 0.0 copy-start
  6.5 0.0 all-gather.4.cloned.1.call-start
  6.5 0.7 all-gather.4.cloned.1.call-update
  7.3 0.0 all-gather.6.cloned.1.call-start
  7.3 1.0 fusion.33
  8.3 113.9 %all-gather.4.cloned.1.call-done = bf16[3,1024,1024]{2,1,0:T(8,128)(2,1)} async-done(((bf16[3,1024,256]{2,1,0:T(8,128)(2,1)}), bf16[3,1024,1024]{2,1,0:T(8,128)(2,1)}) %all-gather.4.cloned.1.call-update) | async-done | bytes 6291472 | tf_op jit(solution)/shard_map/all_gather | solution.py:68
  122.2 4.1 %fusion.11 = bf16[3,32,2,1024]{3,1,0,2:T(8,128)(2,1)S(1)} fusion(bf16[3,1024,1024]{2,1,0:T(8,128)(2,1)} %all-gather.4.cloned.1.call-done, bf16[2,32,1024]{2,1,0:T(8,128)(2,1)} %param.7, f32[1024]{0:T(1024)} %param.8, f32[2,32]{1,0:T(2,128)S(1)} %add_rsqrt_fusion), kind=kOutput, calls=%fused_computation.11 | convolution fusion | flops 403111936 | bytes 6820096 | tf_op jit(solution)/shard_map/rcd,jde->jcre/dot_general | solution.py:65
  126.3 3.0 %copy.23 = bf16[3,32,2,1024]{1,2,0,3:T(2,128)(2,1)} copy(bf16[3,32,2,1024]{3,1,0,2:T(8,128)(2,1)S(1)} %fusion.11) | data formatting | bytes 786432 | tf_op jit(solution)/shard_map/convert_element_type | solution.py:70
  129.3 2.6 %reshape.39 = bf16[4,2,24576]{2,1,0:T(2,128)(2,1)S(1)} reshape(bf16[1024,3,2,32]{3,2,1,0:T(2,128)(2,1)} %bitcast.58) | data formatting | bytes 786432
  132.0 14.4 %all_to_all.15 = bf16[4,2,24576]{2,1,0:T(2,128)(2,1)S(1)} all-to-all(bf16[4,2,24576]{2,1,0:T(2,128)(2,1)S(1)} %reshape.39), channel_id=1, replica_groups=mesh['tile'=8,'head'=4] {'head'}, dimensions={0} | all-to-all | bytes 786432 | tf_op jit(solution)/shard_map/all_to_all | solution.py:71
  146.4 1.7 reshape.40
  148.0 3.8 %copy.24 = bf16[3,32,2,4,256]{4,2,1,3,0:T(2,128)(2,1)S(1)} copy(bf16[3,32,2,4,256]{1,2,0,4,3:T(2,128)(2,1)} %bitcast.59) | data formatting | bytes 786432 | tf_op jit(solution)/shard_map/all_to_all | solution.py:71
  151.8 0.3 fusion.81
  152.1 0.7 reshape_squeeze.10
  152.8 0.0 all-gather.6.cloned.1.call-update
  152.8 0.0 all-gather.8.cloned.1.call-start
  152.9 0.7 reshape_squeeze.11
  153.6 0.0 all-gather.8.cloned.1.call-update
  153.6 0.0 reduce-scatter.2.cloned.1.call-start
  153.7 0.2 reshape_squeeze.9
  153.9 25.0 %all-gather.6.cloned.1.call-done = bf16[2048,256]{1,0:T(8,128)(2,1)} async-done(((bf16[256,256]{1,0:T(8,128)(2,1)}), bf16[2048,256]{1,0:T(8,128)(2,1)}) %all-gather.6.cloned.1.call-update) | async-done | bytes 1048592 | tf_op jit(solution)/shard_map/all_gather | solution.py:82
  178.9 1.5 copy.25
  180.4 1.3 multiply_reduce_fusion
  181.7 0.0 copy-start.1
  181.7 3.2 %copy-done.1 = f32[4,256,2048]{2,1,0:T(8,128)} copy-done((f32[4,256,2048]{2,1,0:T(8,128)}, f32[4,256,2048]{2,1,0:T(8,128)S(1)}, u32[]{:S(2)}) %copy-start.1) | copy-done | bytes 8388632
  184.9 1.6 fusion
  186.6 0.0 copy-start.2
  186.6 0.0 copy-start.3
  186.6 0.0 copy-start.4
  186.6 17.7 %all-gather.8.cloned.1.call-done = bf16[2048,256]{1,0:T(8,128)(2,1)} async-done(((bf16[256,256]{1,0:T(8,128)(2,1)}), bf16[2048,256]{1,0:T(8,128)(2,1)}) %all-gather.8.cloned.1.call-update) | async-done | bytes 1048592 | tf_op jit(solution)/shard_map/all_gather | solution.py:83
  204.3 1.5 copy.27
  205.8 5.0 %fusion.29 = bf16[256,4,64]{0,2,1:T(8,128)(2,1)S(1)} fusion(bf16[2048,4,64]{0,2,1:T(8,128)(2,1)S(1)} %bitcast.61, f32[4,256,2048]{2,1,0:T(8,128)} %copy-done.1, f32[4,256]{1,0:T(4,128)S(1)} %get-tuple-element.43, f32[256,4]{0,1:T(4,128)S(1)} %bitcast_add_fusion, f32[256,4]{0,1:T(4,128)S(1)} %get-tuple-element.42), kind=kOutput, calls=%fused_computation.17 | convolution fusion | flops 274923520 | bytes 9580544 | tf_op jit(solution)/shard_map/while/body/eval_jaxpr/hqk,khe->hqe/dot_general | solution.py:40
  210.8 0.2 copy.28
  211.0 0.2 reshape.34
  211.2 2.1 convolution_convert_fusion
  213.4 0.0 reduce-scatter.2.cloned.1.call-update
  213.4 17.4 %reduce-scatter.2.cloned.1.call-done = bf16[32,2,1024]{2,0,1:T(8,128)(2,1)} async-done(((bf16[128,2,1024]{2,0,1:T(8,128)(2,1)}), bf16[32,2,1024]{2,0,1:T(8,128)(2,1)}) %reduce-scatter.2.cloned.1.call-update) | async-done | bytes 131088 | tf_op jit(solution)/shard_map/reduce_scatter | solution.py:94
  230.8 0.0 copy-done.2
  230.8 0.9 fusion.36
  231.8 4.5 %collective-permute-start = (bf16[1,32,1024]{2,1,0:T(8,128)(2,1)S(1)}, bf16[1,32,1024]{2,1,0:T(8,128)(2,1)S(1)}, u32[]{:S(2)}, u32[]{:S(2)}) collective-permute-start(bf16[1,32,1024]{2,1,0:T(8,128)(2,1)S(1)} %get-tuple-element.30), channel_id=1, source_target_pairs={{0,4},{4,8},{8,12},{12,16},{16,20},{20,24},{24,28},{1,5},{5,9},{9,... | collective-permute-start | bytes 196616 | tf_op jit(solution)/shard_map/ppermute | solution.py:17
  236.3 1.9 collective-permute-start.1
  238.2 0.0 collective-permute-done
  238.2 4.5 %collective-permute-done.1 = bf16[1,32,1024]{2,1,0:T(8,128)(2,1)S(1)} collective-permute-done((bf16[1,32,1024]{2,1,0:T(8,128)(2,1)S(1)}, bf16[1,32,1024]{2,1,0:T(8,128)(2,1)S(1)}, u32[]{:S(2)}, u32[]{:S(2)}) %collective-permute-start.1) | collective-permute-done | bytes 65568 | tf_op jit(solution)/shard_map/ppermute | solution.py:18
  242.8 4.5 %collective-permute-start.2 = (bf16[4,1,1024]{2,1,0:T(2,128)(2,1)S(1)}, bf16[4,1,1024]{2,1,0:T(2,128)(2,1)S(1)}, u32[]{:S(2)}, u32[]{:S(2)}) collective-permute-start(bf16[4,1,1024]{2,1,0:T(2,128)(2,1)S(1)} %get-tuple-element.20), channel_id=1, source_target_pairs={{0,1},{1,2},{2,3},{4,5},{5,6},{6,7},{8,9},{9,10},{10,11},{12,13},{... | collective-permute-start | bytes 24584 | tf_op jit(solution)/shard_map/ppermute | solution.py:17
  247.4 2.0 collective-permute-start.3
  249.4 0.0 copy-done.3
  249.4 0.0 collective-permute-done.2
  249.4 2.4 collective-permute-done.3
  251.8 0.1 maximum_convert_fusion
  252.0 0.0 copy-done
  252.0 0.0 copy-done.4
  252.0 1.4 fusion.23
  (6 shorter events, 0.1 us)
Async XLA Ops:
  6.5 245.4 %copy-start = (bf16[1024,1024]{1,0:T(8,128)(2,1)S(1)}, bf16[1024,1024]{1,0:T(8,128)(2,1)}, u32[]{:S(2)}) copy-start(bf16[1024,1024]{1,0:T(8,128)(2,1)} %param.13) | copy-start | bytes 6291460
  6.5 115.7 %all-gather.4.cloned.1.call-start = ((), (), s32[]{:S(2)}) async-start(), calls=%async_computation.2 | async-start | bytes 7864320 | tf_op jit(solution)/shard_map/all_gather | solution.py:68
  7.3 171.6 %all-gather.6.cloned.1.call-start = ((), (), s32[]{:S(2)}) async-start(), calls=%async_computation.3 | async-start | bytes 1179648 | tf_op jit(solution)/shard_map/all_gather | solution.py:82
  152.8 51.5 %all-gather.8.cloned.1.call-start = ((), (), s32[]{:S(2)}) async-start(), calls=%async_computation.4 | async-start | bytes 1179648 | tf_op jit(solution)/shard_map/all_gather | solution.py:83
  153.6 77.2 %reduce-scatter.2.cloned.1.call-start = ((), (), s32[]{:S(2)}) async-start(), calls=%async_computation.5 | async-start | bytes 655360 | tf_op jit(solution)/shard_map/reduce_scatter | solution.py:94
  181.7 3.2 %copy-start.1 = (f32[4,256,2048]{2,1,0:T(8,128)}, f32[4,256,2048]{2,1,0:T(8,128)S(1)}, u32[]{:S(2)}) copy-start(f32[4,256,2048]{2,1,0:T(8,128)S(1)} %get-tuple-element.45) | copy-start | bytes 25165828
  186.6 44.3 %copy-start.2 = (bf16[2,32,1024]{2,1,0:T(8,128)(2,1)S(1)}, bf16[2,32,1024]{2,1,0:T(8,128)(2,1)}, u32[]{:S(2)}) copy-start(bf16[2,32,1024]{2,1,0:T(8,128)(2,1)} %param.7) | copy-start | bytes 393220
  186.6 62.8 %copy-start.3 = (f32[3,3,1024]{2,1,0:T(4,128)S(1)}, f32[3,3,1024]{2,1,0:T(4,128)}, u32[]{:S(2)}) copy-start(f32[3,3,1024]{2,1,0:T(4,128)} %param.11) | copy-start | bytes 110596
  186.6 65.4 %copy-start.4 = (f32[1024]{0:T(1024)S(1)}, f32[1024]{0:T(1024)}, u32[]{:S(2)}) copy-start(f32[1024]{0:T(1024)} %param.12) | copy-start | bytes 12292
  231.8 6.4 %collective-permute-start = (bf16[1,32,1024]{2,1,0:T(8,128)(2,1)S(1)}, bf16[1,32,1024]{2,1,0:T(8,128)(2,1)S(1)}, u32[]{:S(2)}, u32[]{:S(2)}) collective-permute-start(bf16[1,32,1024]{2,1,0:T(8,128)(2,1)S(1)} %get-tuple-element.30), channel_id=1, source_target_pairs={{0,4},{4,8},{8,12},{12,16},{16,20},{20,24},{24,28},{1,5},{5,9},{9,... | collective-permute-start | bytes 196616 | tf_op jit(solution)/shard_map/ppermute | solution.py:17
  236.3 6.5 %collective-permute-start.1 = (bf16[1,32,1024]{2,1,0:T(8,128)(2,1)S(1)}, bf16[1,32,1024]{2,1,0:T(8,128)(2,1)S(1)}, u32[]{:S(2)}, u32[]{:S(2)}) collective-permute-start(bf16[1,32,1024]{2,1,0:T(8,128)(2,1)S(1)} %get-tuple-element.32), channel_id=1, source_target_pairs={{4,0},{8,4},{12,8},{16,12},{20,16},{24,20},{28,24},{5,1},{9,5},{13... | collective-permute-start | bytes 196616 | tf_op jit(solution)/shard_map/ppermute | solution.py:18
  242.8 6.6 %collective-permute-start.2 = (bf16[4,1,1024]{2,1,0:T(2,128)(2,1)S(1)}, bf16[4,1,1024]{2,1,0:T(2,128)(2,1)S(1)}, u32[]{:S(2)}, u32[]{:S(2)}) collective-permute-start(bf16[4,1,1024]{2,1,0:T(2,128)(2,1)S(1)} %get-tuple-element.20), channel_id=1, source_target_pairs={{0,1},{1,2},{2,3},{4,5},{5,6},{6,7},{8,9},{9,10},{10,11},{12,13},{... | collective-permute-start | bytes 24584 | tf_op jit(solution)/shard_map/ppermute | solution.py:17
  247.4 4.5 %collective-permute-start.3 = (bf16[4,1,1024]{2,1,0:T(2,128)(2,1)S(1)}, bf16[4,1,1024]{2,1,0:T(2,128)(2,1)S(1)}, u32[]{:S(2)}, u32[]{:S(2)}) collective-permute-start(bf16[4,1,1024]{2,1,0:T(2,128)(2,1)S(1)} %get-tuple-element.28), channel_id=1, source_target_pairs={{1,0},{2,1},{3,2},{5,4},{6,5},{7,6},{9,8},{10,9},{11,10},{13,12},{... | collective-permute-start | bytes 24584 | tf_op jit(solution)/shard_map/ppermute | solution.py:18
Sparse Core Ops, SparseCore 0:
  8.9 113.2 all-gather.3
  153.0 25.8 all-gather.5
  180.8 23.4 all-gather.7
  213.5 17.2 reduce-scatter.1
where the time goes:
time: 260 us
  waiting for transfers between devices  182 us (70%)
  local copies, waits for them, and re-layouts  19.6 us (8%)
  blocking collectives  14.4 us (6%)
  matrix products  14 us (5%)
  between operations  13.3 us (5%)
  starting transfers between devices  13.1 us (5%)
  other arithmetic  3.75 us (1%)
    all_gather x1, waiting for transfers between devices, per_device(): lax.all_gather(w_qkv, 'head', axis=2, tiled=True)  114 us
    all_gather x1, waiting for transfers between devices, per_device(): key_piece = lax.all_gather(keys, 'tile', axis=0, tiled=True)  25 us
    all_gather x1, waiting for transfers between devices, per_device(): value_piece = lax.all_gather(vals, 'tile', axis=0, tiled=True)  17.7 us
    reduce_scatter x1, waiting for transfers between devices, per_device(): lax.psum_scatter(jnp.einsum('crh,hd->crd', attended, w_out, preferred_ele...  17.4 us
    all_to_all x1, blocking collectives, per_device(): lax.all_to_all(all_heads, 'head', split_axis=3, concat_axis=1, tiled=True)  14.4 us
    ppermute x2, starting transfers between devices, with_halo(): before = lax.ppermute(last, axis, up)  9.04 us
    unnamed x12, local copies, waits for them, and re-layouts  7.52 us
    ppermute x2, waiting for transfers between devices, with_halo(): after = lax.ppermute(leading, axis, down)  6.94 us
  transfers between devices with their start and end apart: 8, of which 6 were waited for; matrix products, arithmetic and copies ran while one was open for 2% of the time, Pallas kernels for 0%

commit v1 on v0

--- a/solution.py
+++ b/solution.py
@@ -5,6 +5,24 @@
 from jax.sharding import PartitionSpec as P
 
 HEADS = 16
+
+
+def joined_along(blocks, dim):
+    blocks = jnp.moveaxis(blocks, 0, dim)
+    dims = blocks.shape
+    return blocks.reshape(*dims[:dim], dims[dim] * dims[dim + 1], *dims[dim + 2 :])
+
+
+def collected_by_bits(x, axis):
+    peers = lax.axis_size(axis)
+    blocks = x[None]
+    for level in range(peers.bit_length() - 1):
+        stride = 1 << level
+        other = lax.ppermute(blocks, axis, [(i, i ^ stride) for i in range(peers)])
+        both = jnp.stack([blocks, other])
+        upper = lax.axis_index(axis) >> level & 1
+        blocks = jnp.where(upper == 0, both, both[::-1]).reshape(-1, *x.shape)
+    return blocks
 
 
 def with_halo(x, sides, width):
@@ -80,7 +98,7 @@
     vals = projected[2].reshape(seq_local, local_width)
     start_state = empty_state(local_heads, seq_local, head_dim)
     key_piece = lax.all_gather(keys, "tile", axis=0, tiled=True)
-    value_piece = lax.all_gather(vals, "tile", axis=0, tiled=True)
+    value_piece = joined_along(collected_by_bits(vals, "tile"), 0)
     count = key_piece.shape[0]
     maxes, totals, summed = fold_blocks(
         start_state,

time: 260 us -> 242 us (0.931)
  waiting for transfers between devices: 182 us -> 163 us
  matrix products: 14 us -> 9.63 us
  starting transfers between devices: 13.1 us -> 16.9 us
    all_gather x1, waiting for transfers between devices: 25 us -> 0.01 us  [per_device(): key_piece = lax.all_gather(keys, 'tile', axis=0, tiled=True)]
    ppermute x0 -> x3, waiting for transfers between devices: none -> 21.8 us  [collected_by_bits(): other = lax.ppermute(blocks, axis, [(i, i ^ stride) for i in range(peers)])]
    all_gather x1 -> x0, waiting for transfers between devices: 17.7 us -> none  [per_device(): value_piece = lax.all_gather(vals, 'tile', axis=0, tiled=True)]
    ppermute x0 -> x3, starting transfers between devices: none -> 3.92 us  [collected_by_bits(): other = lax.ppermute(blocks, axis, [(i, i ^ stride) for i in range(peers)])]
    dot_general x1, matrix products: 5.01 us -> 1.67 us  [one_block(): jnp.einsum('hqk,khe->hqe', weights.astype(jnp.bfloat16), value_block, pre...]
    unnamed x12 -> x14, local copies, waits for them, and re-layouts: 7.52 us -> 4.32 us
    squeeze x0 -> x1, local copies, waits for them, and re-layouts: none -> 2.61 us  [fold_blocks(): return lax.scan(one_block, state, (key_blocks, value_blocks))[0]]
  transfers between devices with their start and end apart: 8 -> 10, of which waited for: 6 -> 7; matrix products, arithmetic and copies ran while one was open for 2% -> 3% of each run, Pallas kernels for 0% -> 0%
where the time goes in v1:
time: 242 us; the launch traced here: 241 us
  waiting for transfers between devices  163 us (67%)
  local copies, waits for them, and re-layouts  18.7 us (8%)
  starting transfers between devices  16.9 us (7%)
  blocking collectives  14.4 us (6%)
  between operations  13.4 us (6%)
  matrix products  9.63 us (4%)
  other arithmetic  5.34 us (2%)
    all_gather x1, waiting for transfers between devices, per_device(): lax.all_gather(w_qkv, 'head', axis=2, tiled=True)  114 us
    ppermute x3, waiting for transfers between devices, collected_by_bits(): other = lax.ppermute(blocks, axis, [(i, i ^ stride) for i in range(peers)])  21.8 us
    reduce_scatter x1, waiting for transfers between devices, per_device(): lax.psum_scatter(jnp.einsum('crh,hd->crd', attended, w_out, preferred_ele...  19.6 us
    all_to_all x1, blocking collectives, per_device(): lax.all_to_all(all_heads, 'head', split_axis=3, concat_axis=1, tiled=True)  14.4 us
    ppermute x2, starting transfers between devices, with_halo(): before = lax.ppermute(last, axis, up)  9.01 us
    ppermute x2, waiting for transfers between devices, with_halo(): after = lax.ppermute(leading, axis, down)  6.95 us
  transfers between devices with their start and end apart: 10, of which 7 were waited for; matrix products, arithmetic and copies ran while one was open for 3% of the time, Pallas kernels for 0%

profile of v1, /device:TPU:11, one launch (start us, length us, event | category | flops | bytes accessed | tf_op | source)
XLA Modules:
  0.0 241.4 jit_solution(17026880792840460041)
XLA Ops:
  6.5 0.0 copy-start
  6.5 0.0 all-gather.3.cloned.1.call-start
  6.5 0.7 all-gather.3.cloned.1.call-update
  7.3 0.0 all-gather.5.cloned.1.call-start
  7.3 1.0 fusion.33
  8.3 113.9 %all-gather.3.cloned.1.call-done = bf16[3,1024,1024]{2,1,0:T(8,128)(2,1)} async-done(((bf16[3,1024,256]{2,1,0:T(8,128)(2,1)}), bf16[3,1024,1024]{2,1,0:T(8,128)(2,1)}) %all-gather.3.cloned.1.call-update) | async-done | bytes 6291472 | tf_op jit(solution)/shard_map/all_gather | solution.py:86
  122.2 4.1 %fusion.11 = bf16[3,32,2,1024]{3,1,0,2:T(8,128)(2,1)S(1)} fusion(bf16[3,1024,1024]{2,1,0:T(8,128)(2,1)} %all-gather.3.cloned.1.call-done, bf16[2,32,1024]{2,1,0:T(8,128)(2,1)} %param.7, f32[1024]{0:T(1024)} %param.8, f32[2,32]{1,0:T(2,128)S(1)} %add_rsqrt_fusion), kind=kOutput, calls=%fused_computation.12 | convolution fusion | flops 403111936 | bytes 6820096 | tf_op jit(solution)/shard_map/rcd,jde->jcre/dot_general | solution.py:83
  126.3 3.0 %copy.24 = bf16[3,32,2,1024]{1,2,0,3:T(2,128)(2,1)} copy(bf16[3,32,2,1024]{3,1,0,2:T(8,128)(2,1)S(1)} %fusion.11) | data formatting | bytes 786432 | tf_op jit(solution)/shard_map/convert_element_type | solution.py:88
  129.3 2.6 %reshape.48 = bf16[4,2,24576]{2,1,0:T(2,128)(2,1)S(1)} reshape(bf16[1024,3,2,32]{3,2,1,0:T(2,128)(2,1)} %bitcast.68) | data formatting | bytes 786432
  131.9 14.4 %all_to_all.15 = bf16[4,2,24576]{2,1,0:T(2,128)(2,1)S(1)} all-to-all(bf16[4,2,24576]{2,1,0:T(2,128)(2,1)S(1)} %reshape.48), channel_id=1, replica_groups=mesh['tile'=8,'head'=4] {'head'}, dimensions={0} | all-to-all | bytes 786432 | tf_op jit(solution)/shard_map/all_to_all | solution.py:89
  146.3 1.7 reshape.49
  148.0 3.8 %copy.25 = bf16[3,32,2,4,256]{4,2,1,3,0:T(2,128)(2,1)S(1)} copy(bf16[3,32,2,4,256]{1,2,0,4,3:T(2,128)(2,1)} %bitcast.69) | data formatting | bytes 786432 | tf_op jit(solution)/shard_map/all_to_all | solution.py:89
  151.7 0.3 fusion.83
  152.1 0.1 broadcast_in_dim_reshape_squeeze.3
  152.1 2.4 collective-permute-start
  154.5 0.1 stack_broadcast_in_dim_reshape_squeeze.3
  154.6 0.7 reshape_squeeze.7
  155.3 0.0 all-gather.5.cloned.1.call-update
  155.3 0.0 reduce-scatter.2.cloned.1.call-start
  155.4 0.1 collective-permute-done
  155.6 0.1 fusion.57
  155.6 0.3 collective-permute-start.1
  155.9 7.3 %collective-permute-done.1 = bf16[2,256,256]{2,1,0:T(8,128)(2,1)S(1)} collective-permute-done((bf16[2,256,256]{2,1,0:T(8,128)(2,1)S(1)}, bf16[2,256,256]{2,1,0:T(8,128)(2,1)S(1)}, u32[]{:S(2)}, u32[]{:S(2)}) %collective-permute-start.1) | collective-permute-done | bytes 262176 | tf_op jit(solution)/shard_map/ppermute | solution.py:21
  163.2 0.1 pad_maximum_fusion.1
  163.3 0.1 reverse_select_fusion.1
  163.4 1.3 collective-permute-start.2
  164.6 0.2 reshape_squeeze.6
  164.9 14.3 %collective-permute-done.2 = bf16[4,256,256]{2,1,0:T(8,128)(2,1)} collective-permute-done((bf16[4,256,256]{2,1,0:T(8,128)(2,1)S(1)}, bf16[4,256,256]{2,1,0:T(8,128)(2,1)}, u32[]{:S(2)}, u32[]{:S(2)}) %collective-permute-start.2) | collective-permute-done | bytes 524320 | tf_op jit(solution)/shard_map/ppermute | solution.py:21
  179.2 1.1 pad_maximum_fusion
  180.3 0.2 reverse_select_fusion
  180.5 1.8 copy.28
  182.3 2.6 %squeeze.10 = bf16[2048,4,64]{0,2,1:T(8,128)(2,1)} reshape(bf16[2,4,256,256]{2,1,0,3:T(4,128)(2,1)} %copy.28) | data formatting | bytes 2097152 | tf_op jit(solution)/shard_map/while/body/jit(dynamic_index_in_dim)/squeeze | solution.py:66
  184.9 0.0 all-gather.5.cloned.1.call-done
  184.9 1.5 copy.26
  186.4 0.0 copy-start.2
  186.4 1.3 multiply_reduce_fusion
  187.8 0.0 copy-start.3
  187.8 1.6 fusion
  189.4 0.0 copy-start.1
  189.4 0.0 copy-start.4
  189.5 0.0 copy-start.5
  189.5 0.0 copy-done.2
  189.5 1.7 fusion.29
  191.2 0.2 copy.29
  191.4 0.2 reshape.43
  191.6 0.0 copy-done.3
  191.6 1.1 convolution_convert_fusion
  192.7 0.0 reduce-scatter.2.cloned.1.call-update
  192.7 19.6 %reduce-scatter.2.cloned.1.call-done = bf16[32,2,1024]{2,0,1:T(8,128)(2,1)} async-done(((bf16[128,2,1024]{2,0,1:T(8,128)(2,1)}), bf16[32,2,1024]{2,0,1:T(8,128)(2,1)}) %reduce-scatter.2.cloned.1.call-update) | async-done | bytes 131088 | tf_op jit(solution)/shard_map/reduce_scatter | solution.py:112
  212.3 0.0 copy-done.1
  212.3 0.9 fusion.36
  213.3 4.5 %collective-permute-start.3 = (bf16[1,32,1024]{2,1,0:T(8,128)(2,1)S(1)}, bf16[1,32,1024]{2,1,0:T(8,128)(2,1)S(1)}, u32[]{:S(2)}, u32[]{:S(2)}) collective-permute-start(bf16[1,32,1024]{2,1,0:T(8,128)(2,1)S(1)} %get-tuple-element.33), channel_id=1, source_target_pairs={{0,4},{4,8},{8,12},{12,16},{16,20},{20,24},{24,28},{1,5},{5,9},{9,... | collective-permute-start | bytes 196616 | tf_op jit(solution)/shard_map/ppermute | solution.py:35
  217.7 1.9 collective-permute-start.4
  219.7 0.0 collective-permute-done.3
  219.7 4.5 %collective-permute-done.4 = bf16[1,32,1024]{2,1,0:T(8,128)(2,1)S(1)} collective-permute-done((bf16[1,32,1024]{2,1,0:T(8,128)(2,1)S(1)}, bf16[1,32,1024]{2,1,0:T(8,128)(2,1)S(1)}, u32[]{:S(2)}, u32[]{:S(2)}) %collective-permute-start.4) | collective-permute-done | bytes 65568 | tf_op jit(solution)/shard_map/ppermute | solution.py:36
  224.3 4.5 %collective-permute-start.5 = (bf16[4,1,1024]{2,1,0:T(2,128)(2,1)S(1)}, bf16[4,1,1024]{2,1,0:T(2,128)(2,1)S(1)}, u32[]{:S(2)}, u32[]{:S(2)}) collective-permute-start(bf16[4,1,1024]{2,1,0:T(2,128)(2,1)S(1)} %get-tuple-element.20), channel_id=1, source_target_pairs={{0,1},{1,2},{2,3},{4,5},{5,6},{6,7},{8,9},{9,10},{10,11},{12,13},{... | collective-permute-start | bytes 24584 | tf_op jit(solution)/shard_map/ppermute | solution.py:35
  228.8 2.0 collective-permute-start.6
  230.8 0.0 copy-done.4
  230.9 0.0 collective-permute-done.5
  230.9 2.4 collective-permute-done.6
  233.3 0.1 maximum_convert_fusion
  233.4 0.0 copy-done
  233.4 0.0 copy-done.5
  233.4 1.4 fusion.23
  (7 shorter events, 0.1 us)
Async XLA Ops:
  6.5 226.9 %copy-start = (bf16[1024,1024]{1,0:T(8,128)(2,1)S(1)}, bf16[1024,1024]{1,0:T(8,128)(2,1)}, u32[]{:S(2)}) copy-start(bf16[1024,1024]{1,0:T(8,128)(2,1)} %param.13) | copy-start | bytes 6291460
  6.5 115.7 %all-gather.3.cloned.1.call-start = ((), (), s32[]{:S(2)}) async-start(), calls=%async_computation.2 | async-start | bytes 7864320 | tf_op jit(solution)/shard_map/all_gather | solution.py:86
  7.3 177.7 %all-gather.5.cloned.1.call-start = ((), (), s32[]{:S(2)}) async-start(), calls=%async_computation.3 | async-start | bytes 1179648 | tf_op jit(solution)/shard_map/all_gather | solution.py:100
  152.1 3.4 %collective-permute-start = (bf16[1,256,256]{2,1,0:T(8,128)(2,1)S(1)}, bf16[1,256,256]{2,1,0:T(8,128)(2,1)S(1)}, u32[]{:S(2)}, u32[]{:S(2)}) collective-permute-start(bf16[1,256,256]{2,1,0:T(8,128)(2,1)S(1)} %broadcast_in_dim_reshape_squeeze.3), channel_id=1, source_target_pairs={{0,4},{4,0},{8,12},{12,8},{16,20},{20,16},{24,28},{28,24},{1,5},{5... | collective-permute-start | bytes 393224 | tf_op jit(solution)/shard_map/ppermute | solution.py:21
  155.3 57.0 %reduce-scatter.2.cloned.1.call-start = ((), (), s32[]{:S(2)}) async-start(), calls=%async_computation.4 | async-start | bytes 655360 | tf_op jit(solution)/shard_map/reduce_scatter | solution.py:112
  155.6 7.6 %collective-permute-start.1 = (bf16[2,256,256]{2,1,0:T(8,128)(2,1)S(1)}, bf16[2,256,256]{2,1,0:T(8,128)(2,1)S(1)}, u32[]{:S(2)}, u32[]{:S(2)}) collective-permute-start(bf16[2,256,256]{2,1,0:T(8,128)(2,1)S(1)} %get-tuple-element.32), channel_id=1, source_target_pairs={{0,8},{4,12},{8,0},{12,4},{16,24},{20,28},{24,16},{28,20},{1,9},{5... | collective-permute-start | bytes 786440 | tf_op jit(solution)/shard_map/ppermute | solution.py:21
  163.4 15.8 %collective-permute-start.2 = (bf16[4,256,256]{2,1,0:T(8,128)(2,1)S(1)}, bf16[4,256,256]{2,1,0:T(8,128)(2,1)}, u32[]{:S(2)}, u32[]{:S(2)}) collective-permute-start(bf16[4,256,256]{2,1,0:T(8,128)(2,1)S(1)} %bitcast.70), channel_id=1, source_target_pairs={{0,16},{4,20},{8,24},{12,28},{16,0},{20,4},{24,8},{28,12},{1,17},{... | collective-permute-start | bytes 1572872 | tf_op jit(solution)/shard_map/ppermute | solution.py:21
  186.4 3.1 %copy-start.2 = (bf16[2048,4,64]{0,2,1:T(8,128)(2,1)S(1)}, bf16[2048,4,64]{0,2,1:T(8,128)(2,1)}, u32[]{:S(2)}) copy-start(bf16[2048,4,64]{0,2,1:T(8,128)(2,1)} %squeeze.10) | copy-start | bytes 3145732
  187.8 3.8 %copy-start.3 = (bf16[256,1024]{1,0:T(8,128)(2,1)S(1)}, bf16[256,1024]{1,0:T(8,128)(2,1)}, u32[]{:S(2)}) copy-start(bf16[256,1024]{1,0:T(8,128)(2,1)} %param.10) | copy-start | bytes 1572868
  189.4 22.9 %copy-start.1 = (bf16[2,32,1024]{2,1,0:T(8,128)(2,1)S(1)}, bf16[2,32,1024]{2,1,0:T(8,128)(2,1)}, u32[]{:S(2)}) copy-start(bf16[2,32,1024]{2,1,0:T(8,128)(2,1)} %param.7) | copy-start | bytes 393220
  189.4 41.4 %copy-start.4 = (f32[3,3,1024]{2,1,0:T(4,128)S(1)}, f32[3,3,1024]{2,1,0:T(4,128)}, u32[]{:S(2)}) copy-start(f32[3,3,1024]{2,1,0:T(4,128)} %param.11) | copy-start | bytes 110596
  189.5 44.0 %copy-start.5 = (f32[1024]{0:T(1024)S(1)}, f32[1024]{0:T(1024)}, u32[]{:S(2)}) copy-start(f32[1024]{0:T(1024)} %param.12) | copy-start | bytes 12292
  213.3 6.4 %collective-permute-start.3 = (bf16[1,32,1024]{2,1,0:T(8,128)(2,1)S(1)}, bf16[1,32,1024]{2,1,0:T(8,128)(2,1)S(1)}, u32[]{:S(2)}, u32[]{:S(2)}) collective-permute-start(bf16[1,32,1024]{2,1,0:T(8,128)(2,1)S(1)} %get-tuple-element.33), channel_id=1, source_target_pairs={{0,4},{4,8},{8,12},{12,16},{16,20},{20,24},{24,28},{1,5},{5,9},{9,... | collective-permute-start | bytes 196616 | tf_op jit(solution)/shard_map/ppermute | solution.py:35
  217.7 6.5 %collective-permute-start.4 = (bf16[1,32,1024]{2,1,0:T(8,128)(2,1)S(1)}, bf16[1,32,1024]{2,1,0:T(8,128)(2,1)S(1)}, u32[]{:S(2)}, u32[]{:S(2)}) collective-permute-start(bf16[1,32,1024]{2,1,0:T(8,128)(2,1)S(1)} %get-tuple-element.34), channel_id=1, source_target_pairs={{4,0},{8,4},{12,8},{16,12},{20,16},{24,20},{28,24},{5,1},{9,5},{13... | collective-permute-start | bytes 196616 | tf_op jit(solution)/shard_map/ppermute | solution.py:36
  224.3 6.6 %collective-permute-start.5 = (bf16[4,1,1024]{2,1,0:T(2,128)(2,1)S(1)}, bf16[4,1,1024]{2,1,0:T(2,128)(2,1)S(1)}, u32[]{:S(2)}, u32[]{:S(2)}) collective-permute-start(bf16[4,1,1024]{2,1,0:T(2,128)(2,1)S(1)} %get-tuple-element.20), channel_id=1, source_target_pairs={{0,1},{1,2},{2,3},{4,5},{5,6},{6,7},{8,9},{9,10},{10,11},{12,13},{... | collective-permute-start | bytes 24584 | tf_op jit(solution)/shard_map/ppermute | solution.py:35
  228.8 4.5 %collective-permute-start.6 = (bf16[4,1,1024]{2,1,0:T(2,128)(2,1)S(1)}, bf16[4,1,1024]{2,1,0:T(2,128)(2,1)S(1)}, u32[]{:S(2)}, u32[]{:S(2)}) collective-permute-start(bf16[4,1,1024]{2,1,0:T(2,128)(2,1)S(1)} %get-tuple-element.28), channel_id=1, source_target_pairs={{1,0},{2,1},{3,2},{5,4},{6,5},{7,6},{9,8},{10,9},{11,10},{13,12},{... | collective-permute-start | bytes 24584 | tf_op jit(solution)/shard_map/ppermute | solution.py:36
Sparse Core Ops, SparseCore 0:
  8.9 113.2 all-gather.2
  155.5 27.0 all-gather.4
  192.8 19.4 reduce-scatter.1
